TPU v7x, 128 devices: a whole 4x4x4 slice. The times are simulated.
128 devices in a mesh: dp: 4 (over z), expert: 32 (over y, x, core).
Axes of the slice: x: 4, y: 4, z: 4, core: 2. Of those that a mesh axis runs over, the one named last changes fastest.
Arguments:
- tokens: bfloat16 [16384, 3584], P(('dp', 'expert')), may hold values from -6 to 6
- cotangent: bfloat16 [16384, 3584], P(('dp', 'expert')), may hold values from -6 to 6
- gates: bfloat16 [16384, 2], P(('dp', 'expert')), may hold values from 0.099609375 to 1
- expert_ids: int32 [16384, 2], P(('dp', 'expert')), may hold values from 0 to 31, all different within a row; in each aligned block of 128 rows (0 to 127, 128 to 255, ...) at most 10 rows name the same one
- w_gate: bfloat16 [32, 3584, 1024], P('expert', 'dp'), may hold values from -0.09375 to 0.09375
- w_up: bfloat16 [32, 3584, 1024], P('expert', 'dp'), may hold values from -0.09375 to 0.09375
- w_down: bfloat16 [32, 1024, 3584], P('expert', None, 'dp'), may hold values from -0.1875 to 0.1875
- hot_experts: int32 [32], replicated, may hold values from 0 to 31, each once
- copy_counts: int32 [128, 32], P(('dp', 'expert')), may hold values from 0 to 2
Outputs:
- d_tokens: bfloat16 [16384, 3584], P(('dp', 'expert'))
- d_gates: bfloat16 [16384, 2], P(('dp', 'expert'))
- grad_gate: bfloat16 [32, 3584, 1024], P('expert', 'dp')
- grad_up: bfloat16 [32, 3584, 1024], P('expert', 'dp')
- grad_down: bfloat16 [32, 1024, 3584], P('expert', None, 'dp')
- loads: float32 [4, 32], P('dp', 'expert')
Inputs may be any that keep to these rules, and one draw needn't show every extreme that they name: `expert_ids`: in the rows of one device no expert is named by more than 10 rows, a bound that some block reaches. `hot_experts`: each expert exactly once.
All inputs are finite; a program needn't handle non-finite values.
Results may differ from a plain program's by a relative error of at most 0.03.
Values may be sent and summed in bfloat16 or wider, within the bound.
No kernel may reach another device: no remote copies, remote signals or barrier semaphores. Data moves between devices by JAX's collectives and lax.ppermute only.
A program may use at most 128 MiB of HBM per device.

v0:
```python
import math

import jax
import jax.numpy as jnp
from jax import lax
from jax.sharding import PartitionSpec as P

CAPC = 2


def shifted(value, axis, steps):
    count = lax.axis_size(axis)
    pairs = [(source, (source + steps) % count) for source in range(count)]
    return lax.ppermute(value, axis, pairs)


def routing_plan(picked, asked_rows, hot_list, expert_count):
    columns = jnp.arange(expert_count, dtype=jnp.int32)
    onehot = (picked[:, None] == columns[None, :]).astype(jnp.int32)
    earlier = jnp.cumsum(onehot, axis=0) - onehot
    order_rank = jnp.sum(earlier * onehot, axis=1)
    named_count = jnp.sum(onehot, axis=0)
    hot_match = (hot_list[:, None] == columns[None, :]).astype(jnp.int32)
    wanted = jnp.sum(hot_match * asked_rows[:, None], axis=0)
    used_rows = jnp.minimum(wanted, named_count)
    used_per_row = jnp.sum(onehot * used_rows[None, :], axis=1)
    to_copy = order_rank < used_per_row
    return (order_rank, named_count, used_rows, used_per_row, to_copy)


def by_class(row_block, split_at, own_slab, other_slab):
    first_part = jnp.dot(row_block[:split_at], own_slab, preferred_element_type=jnp.float32)
    second_part = jnp.dot(row_block[split_at:], other_slab, preferred_element_type=jnp.float32)
    return jnp.concatenate([first_part, second_part], axis=0)


def by_class_t(row_block, split_at, own_slab, other_slab):
    contract = (((1,), (1,)), ((), ()))
    first_part = lax.dot_general(
        row_block[:split_at], own_slab, contract, preferred_element_type=jnp.float32
    )
    second_part = lax.dot_general(
        row_block[split_at:], other_slab, contract, preferred_element_type=jnp.float32
    )
    return jnp.concatenate([first_part, second_part], axis=0)


def activate(gate_pre, up_pre):
    sigmoid = jax.nn.sigmoid(gate_pre)
    active = gate_pre * sigmoid
    return (sigmoid, active, (active * up_pre).astype(jnp.bfloat16))


def pre_grads(d_hidden, gate_pre, up_pre, sigmoid, active):
    d_gate_pre = (d_hidden * up_pre * sigmoid * (1.0 + gate_pre * (1.0 - sigmoid))).astype(
        jnp.bfloat16
    )
    d_up_pre = (d_hidden * active).astype(jnp.bfloat16)
    return (d_gate_pre, d_up_pre)


def slab_grads(rows_in, hidden, d_output, d_gate_pre, d_up_pre, grad_scale):
    outer_dims = (((0,), (0,)), ((), ()))
    grad_g = lax.dot_general(rows_in, d_gate_pre, outer_dims, preferred_element_type=jnp.float32)
    grad_u = lax.dot_general(rows_in, d_up_pre, outer_dims, preferred_element_type=jnp.float32)
    grad_d = lax.dot_general(hidden, d_output, outer_dims, preferred_element_type=jnp.float32)
    return (
        (grad_g * grad_scale).astype(jnp.bfloat16),
        (grad_u * grad_scale).astype(jnp.bfloat16),
        (grad_d * grad_scale).astype(jnp.bfloat16),
    )


def shards(tokens, cotangent, gates, expert_ids, w_gate, w_up, w_down, hot_experts, copy_counts):
    model_width = tokens.shape[1]
    tok_dev = expert_ids.shape[0]
    top_count = expert_ids.shape[1]
    row_count = tok_dev * top_count
    groups = lax.axis_size("dp")
    server_count = lax.axis_size("expert")
    half_way = server_count // 2
    my_index = lax.axis_index("expert")
    grad_scale = 1.0 / math.sqrt(row_count * groups)
    gate_scale = 1.0 / math.sqrt(model_width)
    bound_most = max(2, 5 * row_count // (4 * server_count))
    chosen = expert_ids.reshape(row_count)
    order_rank, named_count, used_rows, used_per_row, to_copy = routing_plan(
        chosen, copy_counts[0], hot_experts, server_count
    )
    capacity = bound_most + CAPC
    position = jnp.where(to_copy, bound_most + order_rank, order_rank - used_per_row)
    target = jnp.where(to_copy, (chosen + half_way) % server_count, chosen)
    slot_index = target * capacity + position
    slot_total = server_count * capacity
    matches = slot_index[None, :] == jnp.arange(slot_total, dtype=jnp.int32)[:, None]
    source_row = jnp.sum(
        jnp.where(matches, jnp.arange(row_count, dtype=jnp.int32)[None, :], 0), axis=1
    )
    filled = jnp.any(matches, axis=1)
    source_tok = source_row // top_count
    send_in = jnp.where(filled[:, None], tokens[source_tok], jnp.zeros((), tokens.dtype))
    send_cot = jnp.where(filled[:, None], cotangent[source_tok], jnp.zeros((), cotangent.dtype))
    gate_flat = gates.reshape(row_count).astype(jnp.float32)
    send_gate = jnp.where(filled, gate_flat[source_row], 0.0).astype(jnp.bfloat16)
    send_gate = jnp.broadcast_to(
        send_gate.reshape(server_count, capacity, 1), (server_count, capacity, groups)
    )
    got_in, got_cot, got_gate = (
        lax.all_to_all(
            lax.all_to_all(
                send_in.reshape(server_count, capacity, model_width),
                "dp",
                split_axis=2,
                concat_axis=1,
                tiled=True,
            ),
            "expert",
            split_axis=0,
            concat_axis=0,
            tiled=True,
        ),
        lax.all_to_all(
            lax.all_to_all(
                send_cot.reshape(server_count, capacity, model_width),
                "dp",
                split_axis=2,
                concat_axis=1,
                tiled=True,
            ),
            "expert",
            split_axis=0,
            concat_axis=0,
            tiled=True,
        ),
        lax.all_to_all(
            lax.all_to_all(send_gate, "dp", split_axis=2, concat_axis=1, tiled=True),
            "expert",
            split_axis=0,
            concat_axis=0,
            tiled=True,
        ),
    )
    own_gate = w_gate[0]
    own_up = w_up[0]
    own_down = w_down[0]
    split_at = server_count * groups * bound_most
    copy_gate, copy_up, copy_down = shifted((own_gate, own_up, own_down), "expert", half_way)

    def reorder(flat_rows):
        four_way = flat_rows.reshape(server_count, groups, capacity, flat_rows.shape[2])
        main_part = four_way[:, :, :bound_most].reshape(-1, flat_rows.shape[2])
        copy_part = four_way[:, :, bound_most:].reshape(-1, flat_rows.shape[2])
        return jnp.concatenate([main_part, copy_part], axis=0)

    def restore(flat_rows):
        width = flat_rows.shape[1]
        main_part = flat_rows[:split_at].reshape(server_count, groups, bound_most, width)
        copy_part = flat_rows[split_at:].reshape(server_count, groups, CAPC, width)
        return jnp.concatenate([main_part, copy_part], axis=2).reshape(
            server_count, groups * capacity, width
        )

    work_in = reorder(got_in)
    work_cot = reorder(got_cot)
    work_gate = reorder(got_gate).reshape(-1).astype(jnp.float32)
    part_gate = by_class(work_in, split_at, own_gate, copy_gate)
    part_up = by_class(work_in, split_at, own_up, copy_up)
    gate_pre, up_pre = (
        lax.psum(part_gate.astype(jnp.bfloat16), "dp").astype(jnp.float32),
        lax.psum(part_up.astype(jnp.bfloat16), "dp").astype(jnp.float32),
    )
    sigmoid, active, hidden = activate(gate_pre, up_pre)
    output = by_class(hidden, split_at, own_down, copy_down)
    cot_float = work_cot.astype(jnp.float32)
    gate_part = jnp.sum(cot_float * output, axis=1)
    d_output = (work_gate[:, None] * cot_float).astype(jnp.bfloat16)
    hidden_part = by_class_t(d_output, split_at, own_down, copy_down)
    d_hidden, gate_total = (
        lax.psum(hidden_part.astype(jnp.bfloat16), "dp").astype(jnp.float32),
        lax.psum(gate_part.astype(jnp.bfloat16), "dp").astype(jnp.float32),
    )
    d_gate_pre, d_up_pre = pre_grads(d_hidden, gate_pre, up_pre, sigmoid, active)
    d_gate_rows = (gate_total * gate_scale).astype(jnp.bfloat16)
    d_rows = by_class_t(d_gate_pre, split_at, own_gate, copy_gate)
    d_rows = (d_rows + by_class_t(d_up_pre, split_at, own_up, copy_up)).astype(jnp.bfloat16)
    main_terms = slab_grads(
        work_in[:split_at],
        hidden[:split_at],
        d_output[:split_at],
        d_gate_pre[:split_at],
        d_up_pre[:split_at],
        grad_scale,
    )
    copy_terms = slab_grads(
        work_in[split_at:],
        hidden[split_at:],
        d_output[split_at:],
        d_gate_pre[split_at:],
        d_up_pre[split_at:],
        grad_scale,
    )
    at_home = shifted((copy_terms[0], copy_terms[1], copy_terms[2]), "expert", half_way)
    summed = (
        main_terms[0].astype(jnp.float32) + at_home[0].astype(jnp.float32),
        main_terms[1].astype(jnp.float32) + at_home[1].astype(jnp.float32),
        main_terms[2].astype(jnp.float32) + at_home[2].astype(jnp.float32),
    )
    back_rows = restore(d_rows)
    back_gate = restore(d_gate_rows[:, None])
    ret_rows, ret_gate = (
        lax.all_to_all(
            lax.all_to_all(back_rows, "dp", split_axis=1, concat_axis=2, tiled=True),
            "expert",
            split_axis=0,
            concat_axis=0,
            tiled=True,
        ),
        lax.all_to_all(
            lax.all_to_all(back_gate, "dp", split_axis=1, concat_axis=2, tiled=True),
            "expert",
            split_axis=0,
            concat_axis=0,
            tiled=True,
        ),
    )
    row_grads = ret_rows.reshape(slot_total, model_width)[slot_index]
    d_tokens = jnp.sum(
        row_grads.reshape(tok_dev, top_count, model_width).astype(jnp.float32), axis=1
    )
    d_gates = ret_gate[:, :, 0].reshape(slot_total)[slot_index].reshape(tok_dev, top_count)
    served = (named_count - used_rows + jnp.roll(used_rows, half_way)).astype(jnp.float32)
    totals = lax.psum(served, "expert")
    load_here = lax.dynamic_slice_in_dim(totals, my_index, 1) / row_count
    return (
        d_tokens.astype(jnp.bfloat16),
        d_gates,
        summed[0].astype(jnp.bfloat16)[None],
        summed[1].astype(jnp.bfloat16)[None],
        summed[2].astype(jnp.bfloat16)[None],
        load_here.reshape(1, 1),
    )


def solution(mesh):
    placed = (
        P(("dp", "expert"), None),
        P(("dp", "expert"), None),
        P(("dp", "expert"), None),
        P(("dp", "expert"), None),
        P("expert", "dp", None),
        P("expert", "dp", None),
        P("expert", None, "dp"),
        P(),
        P(("dp", "expert"), None),
    )
    return jax.shard_map(
        shards,
        mesh=mesh,
        in_specs=placed,
        out_specs=(
            P(("dp", "expert"), None),
            P(("dp", "expert"), None),
            P("expert", "dp", None),
            P("expert", "dp", None),
            P("expert", None, "dp"),
            P("dp", "expert"),
        ),
        check_vma=False,
    )
```

profile of v0, /device:TPU:1, one launch (start us, length us, event | category | flops | bytes accessed | tf_op | source)
XLA Modules:
  0.0 919.5 jit_solution(18159725980545832358)
XLA Ops:
  15.9 5.9 all-to-all-start
  21.8 3.9 gather_fusion.2
  25.6 5.4 gather.26
  31.0 3.9 gather_fusion.1
  34.9 5.3 gather.24
  41.0 8.0 all-to-all-start.1
  49.0 5.3 broadcast_select_fusion.1
  54.3 21.1 %copy.167 = bf16[32,12,3584]{0,1,2:T(8,128)(2,1)} copy(bf16[32,12,3584]{2,1,0:T(8,128)(2,1)} %get-tuple-element.55) | data formatting | bytes 5505024 | tf_op jit(solution)/shard_map/jit(_where)/select_n | solution.py:102
  75.4 13.8 %reshape.403 = bf16[4,2,172032]{2,1,0:T(2,128)(2,1)} reshape(bf16[3584,12,32]{2,1,0:T(8,128)(2,1)} %bitcast.95) | data formatting | bytes 5505024
  89.2 5.1 all-to-all-start.2
  94.3 21.1 %copy.174 = bf16[32,12,3584]{0,1,2:T(8,128)(2,1)} copy(bf16[32,12,3584]{2,1,0:T(8,128)(2,1)} %get-tuple-element.56) | data formatting | bytes 5505024 | tf_op jit(solution)/shard_map/jit(_where)/select_n | solution.py:101
  115.3 13.8 %reshape.399 = bf16[4,2,172032]{2,1,0:T(2,128)(2,1)} reshape(bf16[3584,12,32]{2,1,0:T(8,128)(2,1)} %bitcast.96) | data formatting | bytes 5505024
  129.1 4.6 all-to-all-start.4
  133.7 12.7 %reshape.404 = bf16[3584,12,32]{2,1,0:T(8,128)(2,1)} reshape(bf16[4,2,172032]{2,1,0:T(2,128)(2,1)} %all-to-all-done.2) | data formatting | bytes 5505024
  146.4 16.3 %copy.189 = bf16[32,12,4,896]{3,2,0,1:T(4,128)(2,1)} copy(bf16[32,12,4,896]{0,1,3,2:T(8,128)(2,1)} %bitcast.97) | data formatting | bytes 5505024 | tf_op jit(solution)/shard_map/all_to_all | solution.py:123
  167.2 8.5 all-to-all-start.3
  175.8 12.7 %reshape.400 = bf16[3584,12,32]{2,1,0:T(8,128)(2,1)} reshape(bf16[4,2,172032]{2,1,0:T(2,128)(2,1)} %all-to-all-done.4) | data formatting | bytes 5505024
  188.5 16.2 %copy.190 = bf16[32,12,4,896]{3,2,0,1:T(4,128)(2,1)} copy(bf16[32,12,4,896]{0,1,3,2:T(8,128)(2,1)} %bitcast.98) | data formatting | bytes 5505024 | tf_op jit(solution)/shard_map/all_to_all | solution.py:110
  210.7 7.1 all-to-all-start.5
  217.8 3.1 collective-permute-start
  221.0 2.9 collective-permute-start.1
  227.2 26.1 %all-to-all-done.5 = bf16[32,48,896]{2,1,0:T(8,128)(2,1)} async-done(((bf16[32,48,896]{2,1,0:T(8,128)(2,1)}), bf16[32,48,896]{2,1,0:T(8,128)(2,1)}, u32[]{:S(2)}, u32[]{:S(2)}) %all-to-all-start.5) | async-done | bytes 2752544 | tf_op jit(solution)/shard_map/all_to_all | solution.py:109
  259.6 2.8 copy.172
  262.4 4.1 reshape.336
  269.6 4.4 copy.179
  274.0 5.3 reshape.339
  281.0 10.1 %collective-permute-done = bf16[1024,896]{1,0:T(8,128)(2,1)} collective-permute-done((bf16[1024,896]{1,0:T(8,128)(2,1)}, bf16[1024,896]{1,0:T(8,128)(2,1)}, u32[]{:S(2)}, u32[]{:S(2)}) %collective-permute-start) | collective-permute-done | bytes 1835040 | tf_op jit(solution)/shard_map/ppermute | solution.py:14
  293.4 4.7 convolution_convert_fusion.2
  298.1 32.3 %collective-permute-done.2 = bf16[896,1024]{1,0:T(8,128)(2,1)} collective-permute-done((bf16[896,1024]{1,0:T(8,128)(2,1)}, bf16[896,1024]{1,0:T(8,128)(2,1)}, u32[]{:S(2)}, u32[]{:S(2)}) %collective-permute-start.2) | collective-permute-done | bytes 1835040 | tf_op jit(solution)/shard_map/ppermute | solution.py:14
  335.2 4.6 convolution_convert_fusion
  341.8 4.6 convolution_convert_fusion.1
  346.4 23.3 %collective-permute-done.1 = bf16[896,1024]{1,0:T(8,128)(2,1)} collective-permute-done((bf16[896,1024]{1,0:T(8,128)(2,1)}, bf16[896,1024]{1,0:T(8,128)(2,1)}, u32[]{:S(2)}, u32[]{:S(2)}) %collective-permute-start.1) | collective-permute-done | bytes 1835040 | tf_op jit(solution)/shard_map/ppermute | solution.py:14
  374.0 228.4 %all-reduce.3.cloned.1.call-done = (bf16[1536,1024]{1,0:T(8,128)(2,1)}, bf16[1536,1024]{1,0:T(8,128)(2,1)}, bf16[1536,1024]{1,0:T(8,128)(2,1)}) async-done(((bf16[1536,1024]{1,0:T(8,128)(2,1)}, bf16[1536,1024]{1,0:T(8,128)(2,1)}, bf16[1536,1024]{1,0:T(8,128)(2,1)}), (bf16[1536,1024]{1,0:T(8,128)(2,1)}, bf16[1536,1024]{1,0:T(8,128)(2,1)}, bf16[1536,1024]{1,0:T(8,128)(2,1)})) %all-reduce.3.cloned.1.call-update) | async-done | bytes 9437200 | tf_op jit(solution)/shard_map/psum | solution.py:170
  602.4 7.9 fusion.4
  610.4 5.9 fusion.18
  616.3 5.8 fusion.22
  622.1 3.7 fusion.41
  629.0 5.8 fusion.11
  634.8 3.3 slice.138
  638.3 5.2 reshape.341
  643.6 5.2 fusion.14
  653.0 6.5 psum.38
  662.1 3.4 all-to-all-start.8
  665.5 3.2 pad_maximum_fusion
  668.7 3.1 copy.181
  671.8 4.7 all-to-all-start.6
  676.6 3.0 multiply_convert_fusion.2
  679.6 2.7 collective-permute-start.4
  682.3 2.9 multiply_convert_fusion.4
  686.5 20.6 %all-to-all-done.6 = bf16[32,48,896]{2,0,1:T(8,128)(2,1)} async-done(((bf16[32,48,896]{2,0,1:T(8,128)(2,1)}), bf16[32,48,896]{2,0,1:T(8,128)(2,1)}, u32[]{:S(2)}, u32[]{:S(2)}) %all-to-all-start.6) | async-done | bytes 2752544 | tf_op jit(solution)/shard_map/all_to_all | solution.py:212
  707.1 10.7 %all-to-all-start.9 = ((bf16[32,12,4]{1,2,0:T(4,128)(2,1)}), bf16[32,12,4]{1,2,0:T(4,128)(2,1)S(1)}, u32[]{:S(2)}, u32[]{:S(2)}) async-start(bf16[32,12,4]{1,2,0:T(4,128)(2,1)} %copy.187), calls=%async_computation.9 | async-start | bytes 65536 | tf_op jit(solution)/shard_map/all_to_all | solution.py:218
  718.0 63.2 %psum.39 = f32[32]{0:T(128)S(1)} all-reduce(f32[32]{0:T(128)S(1)} %fusion.58), channel_id=1, replica_groups=mesh['dp'=4,'expert'=32] {'expert'}, use_global_device_ids=true, to_apply=%region_14.15 | all-reduce | flops 32 | bytes 256 | tf_op jit(solution)/shard_map/psum | solution.py:232
  782.4 5.5 copy.191
  787.9 5.8 reshape.392
  793.8 9.5 %all-to-all-start.7 = ((bf16[32,12,3584]{2,1,0:T(8,128)(2,1)}), bf16[32,12,3584]{2,1,0:T(8,128)(2,1)}, u32[]{:S(2)}, u32[]{:S(2)}) async-start(bf16[32,12,3584]{2,1,0:T(8,128)(2,1)} %reshape.392), calls=%async_computation.7 | async-start | bytes 7340032 | tf_op jit(solution)/shard_map/all_to_all | solution.py:211
  803.3 3.3 multiply_convert_fusion
  806.6 3.0 collective-permute-start.5
  812.8 6.3 fusion.27
  819.1 5.5 fusion.26
  824.6 61.5 %collective-permute-done.5 = bf16[1024,896]{1,0:T(8,128)(2,1)} collective-permute-done((bf16[1024,896]{1,0:T(8,128)(2,1)}, bf16[1024,896]{1,0:T(8,128)(2,1)}, u32[]{:S(2)}, u32[]{:S(2)}) %collective-permute-start.5) | collective-permute-done | bytes 1835040 | tf_op jit(solution)/shard_map/ppermute | solution.py:14
  886.1 5.2 fusion.28
  891.4 5.3 reshape.344
  896.7 5.7 gather_fusion.3
  904.4 6.9 reduce_sum.74
  (159 shorter events, 64.9 us)
Async XLA Ops:
  7.2 14.6 %copy-start = (bf16[128,3584]{1,0:T(8,128)(2,1)S(1)}, bf16[128,3584]{1,0:T(8,128)(2,1)}, u32[]{:S(2)}) copy-start(bf16[128,3584]{1,0:T(8,128)(2,1)} %param.9) | copy-start | bytes 2752516
  8.0 3.0 copy-start.16
  8.4 17.2 %copy-start.25 = (s32[32]{0:T(128)}, s32[32]{0:T(128)S(1)}, u32[]{:S(2)}) copy-start(s32[32]{0:T(128)S(1)} %convert_reduce_fusion) | copy-start | bytes 388
  10.1 15.6 %copy-start.20 = (s32[32]{0:T(128)}, s32[32]{0:T(128)S(1)}, u32[]{:S(2)}) copy-start(s32[32]{0:T(128)S(1)} %min.7) | copy-start | bytes 388
  15.9 24.3 %all-to-all-start = ((bf16[4,2,192]{2,1,0:T(2,128)(2,1)}), bf16[4,2,192]{2,1,0:T(2,128)(2,1)S(1)}, u32[]{:S(2)}, u32[]{:S(2)}) async-start(bf16[4,2,192]{2,1,0:T(2,128)(2,1)} %reshape.401), calls=%async_computation | async-start | bytes 8192 | tf_op jit(solution)/shard_map/all_to_all | solution.py:136
  25.6 5.4 copy-start.2
  41.0 48.2 %all-to-all-start.1 = ((bf16[32,48,1]{1,2,0:T(2,128)(2,1)}), bf16[32,48,1]{1,2,0:T(2,128)(2,1)S(1)}, u32[]{:S(2)}, u32[]{:S(2)}) async-start(bf16[32,48,1]{1,2,0:T(2,128)(2,1)} %copy.163), calls=%async_computation.1 | async-start | bytes 32768 | tf_op jit(solution)/shard_map/all_to_all | solution.py:135
  89.2 40.0 %all-to-all-start.2 = ((bf16[4,2,172032]{2,1,0:T(2,128)(2,1)}), bf16[4,2,172032]{2,1,0:T(2,128)(2,1)}, u32[]{:S(2)}, u32[]{:S(2)}) async-start(bf16[4,2,172032]{2,1,0:T(2,128)(2,1)} %reshape.403), calls=%async_computation.2 | async-start | bytes 5505024 | tf_op jit(solution)/shard_map/all_to_all | solution.py:123
  129.1 38.1 %all-to-all-start.4 = ((bf16[4,2,172032]{2,1,0:T(2,128)(2,1)}), bf16[4,2,172032]{2,1,0:T(2,128)(2,1)}, u32[]{:S(2)}, u32[]{:S(2)}) async-start(bf16[4,2,172032]{2,1,0:T(2,128)(2,1)} %reshape.399), calls=%async_computation.4 | async-start | bytes 5505024 | tf_op jit(solution)/shard_map/all_to_all | solution.py:110
  167.2 43.4 %all-to-all-start.3 = ((bf16[32,48,896]{2,1,0:T(8,128)(2,1)}), bf16[32,48,896]{2,1,0:T(8,128)(2,1)}, u32[]{:S(2)}, u32[]{:S(2)}) async-start(bf16[32,48,896]{2,1,0:T(8,128)(2,1)} %copy.170), calls=%async_computation.3 | async-start | bytes 5505024 | tf_op jit(solution)/shard_map/all_to_all | solution.py:122
  210.7 42.6 %all-to-all-start.5 = ((bf16[32,48,896]{2,1,0:T(8,128)(2,1)}), bf16[32,48,896]{2,1,0:T(8,128)(2,1)}, u32[]{:S(2)}, u32[]{:S(2)}) async-start(bf16[32,48,896]{2,1,0:T(8,128)(2,1)} %copy.177), calls=%async_computation.5 | async-start | bytes 5505024 | tf_op jit(solution)/shard_map/all_to_all | solution.py:109
  217.8 384.7 %all-reduce.3.cloned.1.call-start = ((), (), s32[]{:S(2)}) async-start(), calls=%async_computation.10 | async-start | bytes 18874368 | tf_op jit(solution)/shard_map/psum | solution.py:170
  217.8 73.3 %collective-permute-start = (bf16[1024,896]{1,0:T(8,128)(2,1)}, bf16[1024,896]{1,0:T(8,128)(2,1)}, u32[]{:S(2)}, u32[]{:S(2)}) collective-permute-start(bf16[1024,896]{1,0:T(8,128)(2,1)} %bitcast.8), channel_id=1, source_target_pairs={{0,16},{1,17},{2,18},{3,19},{4,20},{5,21},{6,22},{7,23},{8,24},{9,... | collective-permute-start | bytes 5505032 | tf_op jit(solution)/shard_map/ppermute | solution.py:14
  220.9 109.6 %collective-permute-start.2 = (bf16[896,1024]{1,0:T(8,128)(2,1)}, bf16[896,1024]{1,0:T(8,128)(2,1)}, u32[]{:S(2)}, u32[]{:S(2)}) collective-permute-start(bf16[896,1024]{1,0:T(8,128)(2,1)} %bitcast.14), channel_id=1, source_target_pairs={{0,16},{1,17},{2,18},{3,19},{4,20},{5,21},{6,22},{7,23},{8,24},{9,... | collective-permute-start | bytes 5505032 | tf_op jit(solution)/shard_map/ppermute | solution.py:14
  221.0 148.8 %collective-permute-start.1 = (bf16[896,1024]{1,0:T(8,128)(2,1)}, bf16[896,1024]{1,0:T(8,128)(2,1)}, u32[]{:S(2)}, u32[]{:S(2)}) collective-permute-start(bf16[896,1024]{1,0:T(8,128)(2,1)} %bitcast.13), channel_id=1, source_target_pairs={{0,16},{1,17},{2,18},{3,19},{4,20},{5,21},{6,22},{7,23},{8,24},{9,... | collective-permute-start | bytes 5505032 | tf_op jit(solution)/shard_map/ppermute | solution.py:14
  259.6 19.8 %copy-start.9 = (bf16[256,896]{1,0:T(8,128)(2,1)}, bf16[256,896]{1,0:T(8,128)(2,1)S(1)}, u32[]{:S(2)}) copy-start(bf16[256,896]{1,0:T(8,128)(2,1)S(1)} %reshape.337) | copy-start | bytes 1376260
  281.0 17.1 %copy-start.11 = (bf16[1536,896]{1,0:T(8,128)(2,1)}, bf16[1536,896]{1,0:T(8,128)(2,1)S(1)}, u32[]{:S(2)}) copy-start(bf16[1536,896]{1,0:T(8,128)(2,1)S(1)} %fusion.9) | copy-start | bytes 8257540
  293.4 37.1 %copy-start.18 = (bf16[256,896]{1,0:T(8,128)(2,1)S(1)}, bf16[256,896]{1,0:T(8,128)(2,1)}, u32[]{:S(2)}) copy-start(bf16[256,896]{1,0:T(8,128)(2,1)} %reshape.340) | copy-start | bytes 1376260
  332.7 2.5 copy-start.13
  610.4 11.7 %copy-start.8 = (bf16[1536,1024]{1,0:T(8,128)(2,1)}, bf16[1536,1024]{1,0:T(8,128)(2,1)S(1)}, u32[]{:S(2)}) copy-start(bf16[1536,1024]{1,0:T(8,128)(2,1)S(1)} %get-tuple-element.54) | copy-start | bytes 9437188
  610.4 15.4 %copy-start.6 = (bf16[1536,1024]{1,0:T(8,128)(2,1)}, bf16[1536,1024]{1,0:T(8,128)(2,1)S(1)}, u32[]{:S(2)}) copy-start(bf16[1536,1024]{1,0:T(8,128)(2,1)S(1)} %get-tuple-element.53) | copy-start | bytes 9437188
  616.3 11.8 %copy-start.3 = (f32[1280,896]{1,0:T(8,128)}, f32[1280,896]{1,0:T(8,128)S(1)}, u32[]{:S(2)}) copy-start(f32[1280,896]{1,0:T(8,128)S(1)} %fusion.18) | copy-start | bytes 13762564
  622.1 6.0 copy-start.4
  634.8 3.3 copy-start.15
  648.7 2.4 copy-start.10
  662.1 9.8 %all-to-all-start.8 = ((bf16[4,2,192]{2,1,0:T(2,128)(2,1)}), bf16[4,2,192]{2,1,0:T(2,128)(2,1)S(1)}, u32[]{:S(2)}, u32[]{:S(2)}) async-start(bf16[4,2,192]{2,1,0:T(2,128)(2,1)} %reshape.405), calls=%async_computation.8 | async-start | bytes 8192 | tf_op jit(solution)/shard_map/all_to_all | solution.py:219
  671.8 4.7 copy-start.19
  671.8 35.3 %all-to-all-start.6 = ((bf16[32,48,896]{2,0,1:T(8,128)(2,1)}), bf16[32,48,896]{2,0,1:T(8,128)(2,1)}, u32[]{:S(2)}, u32[]{:S(2)}) async-start(bf16[32,48,896]{2,0,1:T(8,128)(2,1)} %bitcast.99), calls=%async_computation.6 | async-start | bytes 5505024 | tf_op jit(solution)/shard_map/all_to_all | solution.py:212
  676.6 8.9 copy-start.21
  676.6 41.2 %copy-start.26 = (s32[32]{0:T(128)S(1)}, s32[32]{0:T(128)}, u32[]{:S(2)}) copy-start(s32[32]{0:T(128)} %copy-done.25) | copy-start | bytes 388
  676.6 41.3 %copy-start.17 = (s32[128,2]{1,0:T(8,128)S(1)}, s32[128,2]{1,0:T(8,128)}, u32[]{:S(2)}) copy-start(s32[128,2]{1,0:T(8,128)} %copy-done.16) | copy-start | bytes 3076
  679.6 133.2 %collective-permute-start.4 = (bf16[896,1024]{1,0:T(8,128)(2,1)}, bf16[896,1024]{1,0:T(8,128)(2,1)}, u32[]{:S(2)}, u32[]{:S(2)}) collective-permute-start(bf16[896,1024]{1,0:T(8,128)(2,1)} %multiply_convert_fusion.2), channel_id=1, source_target_pairs={{0,16},{1,17},{2,18},{3,19},{4,20},{5,21},{6,22},{7,23},{8,24},{9,... | collective-permute-start | bytes 5505032 | tf_op jit(solution)/shard_map/ppermute | solution.py:14
  685.2 133.8 %collective-permute-start.3 = (bf16[896,1024]{1,0:T(8,128)(2,1)}, bf16[896,1024]{1,0:T(8,128)(2,1)}, u32[]{:S(2)}, u32[]{:S(2)}) collective-permute-start(bf16[896,1024]{1,0:T(8,128)(2,1)} %multiply_convert_fusion.4), channel_id=1, source_target_pairs={{0,16},{1,17},{2,18},{3,19},{4,20},{5,21},{6,22},{7,23},{8,24},{9,... | collective-permute-start | bytes 5505032 | tf_op jit(solution)/shard_map/ppermute | solution.py:14
  707.1 86.6 %all-to-all-start.9 = ((bf16[32,12,4]{1,2,0:T(4,128)(2,1)}), bf16[32,12,4]{1,2,0:T(4,128)(2,1)S(1)}, u32[]{:S(2)}, u32[]{:S(2)}) async-start(bf16[32,12,4]{1,2,0:T(4,128)(2,1)} %copy.187), calls=%async_computation.9 | async-start | bytes 65536 | tf_op jit(solution)/shard_map/all_to_all | solution.py:218
  793.8 97.6 %all-to-all-start.7 = ((bf16[32,12,3584]{2,1,0:T(8,128)(2,1)}), bf16[32,12,3584]{2,1,0:T(8,128)(2,1)}, u32[]{:S(2)}, u32[]{:S(2)}) async-start(bf16[32,12,3584]{2,1,0:T(8,128)(2,1)} %reshape.392), calls=%async_computation.7 | async-start | bytes 7340032 | tf_op jit(solution)/shard_map/all_to_all | solution.py:211
  803.3 6.3 copy-start.22
  803.3 6.3 copy-start.23
  803.3 6.3 copy-start.24
  803.3 9.4 %copy-start.14 = (bf16[1280,896]{1,0:T(8,128)(2,1)S(1)}, bf16[1280,896]{1,0:T(8,128)(2,1)}, u32[]{:S(2)}) copy-start(bf16[1280,896]{1,0:T(8,128)(2,1)} %reshape.339) | copy-start | bytes 6881284
  806.6 79.5 %collective-permute-start.5 = (bf16[1024,896]{1,0:T(8,128)(2,1)}, bf16[1024,896]{1,0:T(8,128)(2,1)}, u32[]{:S(2)}, u32[]{:S(2)}) collective-permute-start(bf16[1024,896]{1,0:T(8,128)(2,1)} %multiply_convert_fusion), channel_id=1, source_target_pairs={{0,16},{1,17},{2,18},{3,19},{4,20},{5,21},{6,22},{7,23},{8,24},{9,... | collective-permute-start | bytes 5505032 | tf_op jit(solution)/shard_map/ppermute | solution.py:14
  812.7 6.3 copy-start.7
  819.1 67.1 %copy-start.5 = (bf16[1536,1024]{1,0:T(8,128)(2,1)S(1)}, bf16[1536,1024]{1,0:T(8,128)(2,1)}, u32[]{:S(2)}) copy-start(bf16[1536,1024]{1,0:T(8,128)(2,1)} %get-tuple-element.52) | copy-start | bytes 9437188
  819.1 67.1 %copy-start.12 = (bf16[1536,896]{1,0:T(8,128)(2,1)S(1)}, bf16[1536,896]{1,0:T(8,128)(2,1)}, u32[]{:S(2)}) copy-start(bf16[1536,896]{1,0:T(8,128)(2,1)} %copy-done.11) | copy-start | bytes 8257540
  896.7 14.5 %copy-start.1 = (bf16[128,3584]{1,0:T(8,128)(2,1)S(1)}, bf16[128,3584]{1,0:T(8,128)(2,1)}, u32[]{:S(2)}) copy-start(bf16[128,3584]{1,0:T(8,128)(2,1)} %param.9) | copy-start | bytes 2752516
Sparse Core Ops, SparseCore 0:
  374.1 228.2 all-reduce.2
where the time goes:
time: 930 us; the launch traced here: 920 us
  waiting for transfers between devices  404 us (43%)
  local copies, waits for them, and re-layouts  235 us (25%)
  starting transfers between devices  79.6 us (9%)
  matrix products  72.1 us (8%)
  blocking collectives  69.7 us (7%)
  other arithmetic  42.9 us (5%)
  between operations  16.8 us (2%)
    psum x1, waiting for transfers between devices, shards(): lax.psum(part_up.astype(jnp.bfloat16), 'dp').astype(jnp.float32)  228 us
    ppermute x6, waiting for transfers between devices, shifted(): return lax.ppermute(value, axis, pairs)  127 us
    psum x1, blocking collectives, shards(): totals = lax.psum(served, 'expert')  63.2 us
    unnamed x66, local copies, waits for them, and re-layouts  57.2 us
    all_to_all x1, waiting for transfers between devices, shards(): lax.all_to_all(lax.all_to_all(send_in.reshape(server_count, capacity, mod...  26.1 us
    select_n x1, local copies, waits for them, and re-layouts, shards(): jnp.where(filled[:, None], tokens[source_tok], jnp.zeros((), tokens.dtype))  21.1 us
    select_n x1, local copies, waits for them, and re-layouts, shards(): jnp.where(filled[:, None], cotangent[source_tok], jnp.zeros((), cotangent...  21.1 us
    all_to_all x3, local copies, waits for them, and re-layouts, shards(): lax.all_to_all(send_cot.reshape(server_count, capacity, model_width), 'dp...  20.8 us
  transfers between devices with their start and end apart: 17, of which 8 were waited for; matrix products, arithmetic and copies ran while one was open for 29% of the time, Pallas kernels for 0%

commit v1 on v0

v1 whole, which is shorter than its diff:
```python
import math

import jax
import jax.numpy as jnp
from jax import lax
from jax.sharding import PartitionSpec as P

MOST = 10


def routing_plan(picked, asked_rows, hot_list, expert_count):
    rows = picked.shape[0]
    place = jnp.arange(rows, dtype=jnp.int32)
    earlier = (picked[:, None] == picked[None, :]) & (place[None, :] < place[:, None])
    order_rank = jnp.sum(earlier.astype(jnp.int32), axis=1)
    columns = jnp.arange(expert_count, dtype=jnp.int32)
    onehot = (picked[:, None] == columns[None, :]).astype(jnp.int32)
    named_count = jnp.sum(onehot, axis=0)
    hot_match = (hot_list[:, None] == columns[None, :]).astype(jnp.int32)
    wanted = jnp.sum(hot_match * asked_rows[:, None], axis=0)
    used_rows = jnp.minimum(wanted, named_count)
    return order_rank, named_count, used_rows


def to_quarters(value, groups):
    rows, width = value.shape
    parts = value.reshape(rows, groups, width // groups).transpose(1, 0, 2)
    got = lax.all_to_all(parts, "dp", 0, 0, tiled=True)
    return got.reshape(groups * rows, width // groups)


def from_quarters(value, groups):
    rows, width = value.shape[0] // groups, value.shape[1]
    got = lax.all_to_all(value.reshape(groups, rows, width), "dp", 0, 0, tiled=True)
    return got.transpose(1, 0, 2).reshape(rows, groups * width)


def over_experts(value):
    return lax.all_to_all(value, "expert", 0, 0, tiled=True)


def shards(tokens, cotangent, gates, expert_ids, w_gate, w_up, w_down, hot_experts, copy_counts):
    model_width = tokens.shape[1]
    tok_dev, top_count = expert_ids.shape
    row_count = tok_dev * top_count
    groups = lax.axis_size("dp")
    servers = lax.axis_size("expert")
    group = lax.axis_index("dp")
    grad_scale = 1.0 / math.sqrt(row_count * groups)
    gate_scale = 1.0 / math.sqrt(model_width)
    per_pair = groups * MOST
    slots = servers * per_pair
    own_slots = slots // groups
    f32, bf16 = jnp.float32, jnp.bfloat16

    chosen = expert_ids.reshape(row_count)
    order_rank, named_count, used_rows = routing_plan(chosen, copy_counts[0], hot_experts, servers)
    slot_row = chosen * per_pair + group * MOST + order_rank
    plan = jnp.stack([slot_row.astype(f32), gates.reshape(row_count).astype(f32)])
    plan = lax.all_gather(plan, "dp", axis=0)
    tok_q = to_quarters(tokens, groups)
    cot_q = to_quarters(cotangent, groups)

    slot_of = plan[:, 0].astype(jnp.int32).reshape(groups * tok_dev, top_count)
    gate_of = plan[:, 1].reshape(groups * tok_dev, top_count)
    slot_ids = jnp.arange(slots, dtype=jnp.int32)[:, None]
    hits = [slot_ids == slot_of[None, :, k] for k in range(top_count)]
    dispatch = hits[0]
    for hit in hits[1:]:
        dispatch = dispatch | hit
    dispatch = dispatch.astype(bf16)
    slot_gate = sum(
        jnp.sum(jnp.where(hit, gate_of[None, :, k], 0.0), axis=1) for k, hit in enumerate(hits)
    )
    served = (named_count - used_rows + jnp.roll(used_rows, servers // 2)).astype(f32)
    small = jnp.concatenate([slot_gate.reshape(servers, per_pair), served[:, None]], axis=1)
    small = over_experts(small)
    load_here = jnp.sum(small[:, per_pair]) / row_count
    row_gate = small[:, :per_pair].reshape(slots)
    row_gate = lax.dynamic_slice_in_dim(row_gate, group * own_slots, own_slots)[:, None]

    send_in = jnp.dot(dispatch, tok_q, preferred_element_type=f32).astype(bf16)
    send_cot = jnp.dot(dispatch, cot_q, preferred_element_type=f32).astype(bf16)
    rows_in = over_experts(send_in)
    rows_cot = over_experts(send_cot)

    w_both = jnp.concatenate([w_gate[0], w_up[0]], axis=1)
    hidden_width = w_gate.shape[2]
    own_down = w_down[0]
    across = (((1,), (1,)), ((), ()))
    pre_part = jnp.dot(rows_in, w_both, preferred_element_type=f32).astype(bf16)
    pre = lax.psum_scatter(pre_part, "dp", scatter_dimension=0, tiled=True).astype(f32)
    back_part = lax.dot_general(rows_cot, own_down, across, preferred_element_type=f32).astype(bf16)
    back = lax.psum_scatter(back_part, "dp", scatter_dimension=0, tiled=True).astype(f32)

    gate_pre, up_pre = pre[:, :hidden_width], pre[:, hidden_width:]
    sigmoid = jax.nn.sigmoid(gate_pre)
    active = gate_pre * sigmoid
    hidden = active * up_pre
    d_gate_rows = jnp.sum(hidden * back, axis=1) * gate_scale
    d_hidden = row_gate * back
    d_gate_pre = d_hidden * up_pre * sigmoid * (1.0 + gate_pre * (1.0 - sigmoid))
    d_up_pre = d_hidden * active
    d_both = jnp.concatenate([d_gate_pre.astype(bf16), d_up_pre.astype(bf16)], axis=1)
    gated = (hidden * row_gate).astype(bf16)

    d_both = lax.all_gather(d_both, "dp", axis=0, tiled=True)
    gated = lax.all_gather(gated, "dp", axis=0, tiled=True)
    d_gate_all = lax.all_gather(d_gate_rows[None], "dp", axis=0, tiled=True)

    d_rows = lax.dot_general(d_both, w_both, across, preferred_element_type=f32).astype(bf16)
    back_rows = over_experts(d_rows)
    back_gate = over_experts(d_gate_all.reshape(servers, per_pair))

    outer = (((0,), (0,)), ((), ()))
    grad_both = [
        (lax.dot_general(rows_in, part, outer, preferred_element_type=f32) * grad_scale).astype(bf16)
        for part in (d_both[:, :hidden_width], d_both[:, hidden_width:])
    ]
    grad_down = lax.dot_general(gated, rows_cot, outer, preferred_element_type=f32)
    grad_down = (grad_down * grad_scale).astype(bf16)

    d_tok_q = lax.dot_general(dispatch, back_rows, outer, preferred_element_type=f32).astype(bf16)
    d_tokens = from_quarters(d_tok_q, groups)

    mine = lax.dynamic_slice_in_dim(back_gate, group * MOST, MOST, axis=1).reshape(1, servers * MOST)
    spot = chosen * MOST + order_rank
    match = spot[:, None] == jnp.arange(servers * MOST, dtype=jnp.int32)[None, :]
    d_gates = jnp.sum(jnp.where(match, mine, 0.0), axis=1).astype(bf16).reshape(tok_dev, top_count)
    return (
        d_tokens,
        d_gates,
        grad_both[0][None],
        grad_both[1][None],
        grad_down[None],
        load_here.reshape(1, 1),
    )


def solution(mesh):
    rows = P(("dp", "expert"), None)
    return jax.shard_map(
        shards,
        mesh=mesh,
        in_specs=(
            rows,
            rows,
            rows,
            rows,
            P("expert", "dp", None),
            P("expert", "dp", None),
            P("expert", None, "dp"),
            P(),
            rows,
        ),
        out_specs=(
            rows,
            rows,
            P("expert", "dp", None),
            P("expert", "dp", None),
            P("expert", None, "dp"),
            P("dp", "expert"),
        ),
        check_vma=False,
    )
```

time: 930 us -> 330 us (0.35)
  waiting for transfers between devices: 404 us -> 79.4 us
  local copies, waits for them, and re-layouts: 235 us -> 16.1 us
  blocking collectives: 69.7 us -> 125 us
  starting transfers between devices: 79.6 us -> 30.6 us
  other arithmetic: 42.9 us -> 10.8 us
  matrix products: 72.1 us -> 49.7 us
    psum x1 -> x0, waiting for transfers between devices: 228 us -> none  [shards(): lax.psum(part_up.astype(jnp.bfloat16), 'dp').astype(jnp.float32)]
    ppermute x6 -> x0, waiting for transfers between devices: 127 us -> none  [shifted(): return lax.ppermute(value, axis, pairs)]
    all_to_all x0 -> x3, blocking collectives: none -> 103 us  [the longest x2 75.9 us: over_experts(): return lax.all_to_all(value, 'expert', 0, 0, tiled=True)]
    psum x2 -> x0, blocking collectives: 69.7 us -> none  [the longest x1 63.2 us: shards(): totals = lax.psum(served, 'expert')]
    all_gather x0 -> x2, waiting for transfers between devices: none -> 56.2 us  [the longest x1 38.1 us: shards(): d_both = lax.all_gather(d_both, 'dp', axis=0, tiled=True)]
    all_to_all x17 -> x3, local copies, waits for them, and re-layouts: 59.2 us -> 3.25 us  [the longest x2 2.55 us: to_quarters(): got = lax.all_to_all(parts, 'dp', 0, 0, tiled=True)]
    unnamed x66 -> x30, local copies, waits for them, and re-layouts: 57.2 us -> 9.38 us
    select_n x2 -> x0, local copies, waits for them, and re-layouts: 42.2 us -> none  [the longest x1 21.1 us: shards(): jnp.where(filled[:, None], tokens[source_tok], jnp.zeros((), tokens.dtype))]
  transfers between devices with their start and end apart: 17 -> 9, of which waited for: 8 -> 5; matrix products, arithmetic and copies ran while one was open for 29% -> 15% of each run, Pallas kernels for 0% -> 0%
where the time goes in v1:
time: 330 us; the launch traced here: 328 us
  blocking collectives  125 us (38%)
  waiting for transfers between devices  79.4 us (24%)
  matrix products  49.7 us (15%)
  starting transfers between devices  30.6 us (9%)
  between operations  16.4 us (5%)
  local copies, waits for them, and re-layouts  16.1 us (5%)
  other arithmetic  10.8 us (3%)
    all_to_all x2, blocking collectives, over_experts(): return lax.all_to_all(value, 'expert', 0, 0, tiled=True)  75.9 us
    all_gather x1, waiting for transfers between devices, shards(): d_both = lax.all_gather(d_both, 'dp', axis=0, tiled=True)  38.1 us
    all_to_all x1, blocking collectives, to_quarters(): got = lax.all_to_all(parts, 'dp', 0, 0, tiled=True)  27.5 us
    all_to_all x3, starting transfers between devices, over_experts(): return lax.all_to_all(value, 'expert', 0, 0, tiled=True)  20.9 us
    all_gather x1, waiting for transfers between devices, shards(): gated = lax.all_gather(gated, 'dp', axis=0, tiled=True)  18.1 us
    all_gather x1, blocking collectives, shards(): plan = lax.all_gather(plan, 'dp', axis=0)  14.6 us
    reduce_scatter x1, waiting for transfers between devices, shards(): lax.psum_scatter(back_part, 'dp', scatter_dimension=0, tiled=True)  12.8 us
    dot_general x2, matrix products, shards(): lax.dot_general(rows_in, part, outer, preferred_element_type=f32)  12 us
  transfers between devices with their start and end apart: 9, of which 5 were waited for; matrix products, arithmetic and copies ran while one was open for 15% of the time, Pallas kernels for 0%

profile of v1, /device:TPU:1, one launch (start us, length us, event | category | flops | bytes accessed | tf_op | source)
XLA Modules:
  0.0 327.6 jit_solution(15561292390708135641)
XLA Ops:
  7.2 2.3 copy.49
  9.5 5.9 %all-to-all-start.3 = ((bf16[4,128,896]{1,2,0:T(8,128)(2,1)}), bf16[4,128,896]{1,2,0:T(8,128)(2,1)S(1)}, u32[]{:S(2)}, u32[]{:S(2)}) async-start(bf16[4,128,896]{1,2,0:T(8,128)(2,1)} %bitcast.60), calls=%async_computation.4 | async-start | bytes 1835008 | tf_op jit(solution)/shard_map/all_to_all | solution.py:28
  15.4 0.1 copy.44
  15.5 0.1 copy.43
  15.6 0.1 add.68
  15.8 0.1 copy.45
  15.9 0.1 reshape.183
  16.1 0.1 eq.85
  16.2 0.2 convert_reduce_fusion
  16.4 14.6 %all-gather.2 = f32[4,2,256]{2,1,0:T(2,128)S(1)} all-gather(f32[1,2,256]{2,1,0:T(2,128)S(1)} %maximum_bitcast_fusion), channel_id=2, replica_groups=mesh['dp'=4,'expert'=32] {'dp'}, dimensions={0}, use_global_device_ids=true | all-gather | bytes 10240 | tf_op jit(solution)/shard_map/all_gather | solution.py:60
  31.0 0.2 convert_element_type.102
  31.2 0.3 slice_reduce_fusion.3
  31.5 1.3 copy.50
  32.8 2.7 convolution_convert_fusion.3
  35.6 41.4 %all_to_all.72 = bf16[32,40,896]{2,1,0:T(8,128)(2,1)S(1)} all-to-all(bf16[32,40,896]{2,1,0:T(8,128)(2,1)S(1)} %bitcast.69), channel_id=1, replica_groups=mesh['dp'=4,'expert'=32] {'expert'}, dimensions={0} | all-to-all | bytes 4587520 | tf_op jit(solution)/shard_map/all_to_all | solution.py:39
  77.0 1.4 copy-done.1
  78.4 7.5 %convolution_convert_fusion = bf16[1280,2048]{1,0:T(8,128)(2,1)} fusion(bf16[1280,896]{1,0:T(8,128)(2,1)S(1)} %bitcast.63, bf16[896,1024]{1,0:T(8,128)(2,1)S(1)} %bitcast.79, bf16[896,1024]{1,0:T(8,128)(2,1)S(1)} %bitcast.81), kind=kOutput, calls=%fused_computation | convolution fusion | flops 4707581952 | bytes 11206656 | tf_op jit(solution)/shard_map/dot_general | solution.py:91
  86.0 1.1 copy-done.4
  87.1 1.3 copy.47
  88.4 27.5 %all_to_all.73 = bf16[4,128,896]{1,2,0:T(8,128)(2,1)S(1)} all-to-all(bf16[4,128,896]{1,2,0:T(8,128)(2,1)} %bitcast.62), channel_id=1, replica_groups=mesh['dp'=4,'expert'=32] {'dp'}, dimensions={0} | all-to-all | bytes 1835008 | tf_op jit(solution)/shard_map/all_to_all | solution.py:28
  115.9 1.3 copy.48
  117.1 2.7 convolution_convert_fusion.4
  119.8 34.5 %all_to_all.74 = bf16[32,40,896]{2,1,0:T(8,128)(2,1)S(1)} all-to-all(bf16[32,40,896]{2,1,0:T(8,128)(2,1)S(1)} %bitcast.70), channel_id=1, replica_groups=mesh['dp'=4,'expert'=32] {'expert'}, dimensions={0} | all-to-all | bytes 4587520 | tf_op jit(solution)/shard_map/all_to_all | solution.py:39
  154.3 1.4 copy-done.3
  155.7 4.3 %convolution_convert_fusion.1 = bf16[1280,1024]{1,0:T(8,128)(2,1)} fusion(bf16[1280,896]{1,0:T(8,128)(2,1)S(1)} %bitcast.66, bf16[1,1024,896]{2,1,0:T(8,128)(2,1)S(1)} %copy-done), kind=kOutput, calls=%fused_computation.1 | convolution fusion | flops 2350120960 | bytes 6750208 | tf_op jit(solution)/shard_map/dot_general | solution.py:93
  160.0 0.1 convert_reduce_fusion.1
  160.1 0.5 copy-done.9
  160.7 0.1 select_reduce_fusion.3
  160.9 0.1 copy.46
  161.0 0.2 reshape_squeeze.3
  161.3 0.3 slice_reduce_fusion
  161.6 0.7 select_reduce_fusion
  162.2 0.1 add.71
  162.3 0.7 pad_maximum_fusion.4
  163.0 3.8 %all-to-all-start = ((f32[32,1,41]{2,1,0:T(1,128)}), f32[32,1,41]{2,1,0:T(1,128)S(1)}, u32[]{:S(2)}, u32[]{:S(2)}) async-start(f32[32,1,41]{2,1,0:T(1,128)} %bitcast.7), calls=%async_computation | async-start | bytes 32768 | tf_op jit(solution)/shard_map/all_to_all | solution.py:39
  166.9 6.9 %all-to-all-done = f32[32,1,41]{2,1,0:T(1,128)S(1)} async-done(((f32[32,1,41]{2,1,0:T(1,128)}), f32[32,1,41]{2,1,0:T(1,128)S(1)}, u32[]{:S(2)}, u32[]{:S(2)}) %all-to-all-start) | async-done | bytes 5280 | tf_op jit(solution)/shard_map/all_to_all | solution.py:39
  173.9 0.1 dynamic_slice.6
  174.0 3.2 convert_element_type.110
  177.1 12.8 %reduce-scatter.3.cloned.1.call-done = bf16[320,1024]{1,0:T(8,128)(2,1)} async-done(((bf16[1280,1024]{1,0:T(8,128)(2,1)}), bf16[320,1024]{1,0:T(8,128)(2,1)}) %reduce-scatter.3.cloned.1.call-update) | async-done | bytes 655376 | tf_op jit(solution)/shard_map/reduce_scatter | solution.py:94
  189.9 3.7 %fusion.24 = (bf16[320,1024]{1,0:T(8,128)(2,1)S(1)}, bf16[320,1024]{1,0:T(8,128)(2,1)S(1)}, f32[320]{0:T(512)S(1)}, bf16[320,1024]{1,0:T(8,128)(2,1)}) fusion(bf16[320,1024]{1,0:T(8,128)(2,1)} %reduce-scatter.3.cloned.1.call-done, f32[320,2048]{1,0:T(8,128)} %convert_element_type.110, f32[320]{0:T(512)S(1)} %dynamic_slice.6), kind=kLoop, calls=%fused_computation.30 | loop fusion | flops 6553280 | bytes 5245440 | tf_op jit(solution)/shard_map/convert_element_type | solution.py:104
  193.7 1.1 pad_maximum_fusion.3
  194.9 0.5 all-gather.8.cloned.1.call-update
  195.4 0.6 dynamic-slice.1
  196.7 0.1 multiply_dynamic-update-slice_fusion
  196.8 6.6 %all-reduce = f32[1280]{0:T(1024)S(1)} all-reduce(f32[1280]{0:T(1024)S(1)} %multiply_dynamic-update-slice_fusion), channel_id=3, replica_groups=mesh['dp'=4,'expert'=32] {'dp'}, use_global_device_ids=true, to_apply=%add | all-reduce | flops 1280 | bytes 10240
  203.4 0.7 all_to_all.62
  204.1 9.5 %all-to-all-start.7 = ((f32[32,1,40]{2,1,0:T(1,128)}), f32[32,1,40]{2,1,0:T(1,128)S(1)}, u32[]{:S(2)}, u32[]{:S(2)}) async-start(f32[32,1,40]{2,1,0:T(1,128)} %all_to_all.62), calls=%async_computation.9 | async-start | bytes 32768 | tf_op jit(solution)/shard_map/all_to_all | solution.py:39
  213.6 38.1 %all-gather.6.cloned.1.call-done = bf16[1280,2048]{1,0:T(8,128)(2,1)} async-done(((bf16[320,2048]{1,0:T(8,128)(2,1)}), bf16[1280,2048]{1,0:T(8,128)(2,1)}) %all-gather.6.cloned.1.call-update) | async-done | bytes 5242896 | tf_op jit(solution)/shard_map/all_gather | solution.py:107
  251.7 9.7 %convolution_convert_fusion.2 = bf16[1280,896]{1,0:T(8,128)(2,1)} fusion(bf16[1280,2048]{1,0:T(8,128)(2,1)} %all-gather.6.cloned.1.call-done, bf16[896,1024]{1,0:T(8,128)(2,1)} %bitcast.78, bf16[896,1024]{1,0:T(8,128)(2,1)} %bitcast.80), kind=kOutput, calls=%fused_computation.6 | convolution fusion | flops 4706107392 | bytes 11206656 | tf_op jit(solution)/shard_map/dot_general | solution.py:111
  261.4 7.6 %all-to-all-start.5 = ((bf16[32,40,896]{2,1,0:T(8,128)(2,1)}), bf16[32,40,896]{2,1,0:T(8,128)(2,1)}, u32[]{:S(2)}, u32[]{:S(2)}) async-start(bf16[32,40,896]{2,1,0:T(8,128)(2,1)} %bitcast.68), calls=%async_computation.7 | async-start | bytes 4587520 | tf_op jit(solution)/shard_map/all_to_all | solution.py:39
  269.0 0.7 slice_reduce_fusion.4
  270.4 0.1 dynamic-slice_reduce_fusion
  270.5 0.1 broadcast_in_dim.61
  270.6 0.1 select_reduce_fusion.2
  270.7 0.2 convert_element_type.116
  270.9 0.6 copy.52
  271.5 18.1 %all-gather.8.cloned.1.call-done = bf16[1280,1024]{1,0:T(8,128)(2,1)} async-done(((bf16[320,1024]{1,0:T(8,128)(2,1)}), bf16[1280,1024]{1,0:T(8,128)(2,1)}) %all-gather.8.cloned.1.call-update) | async-done | bytes 2621456 | tf_op jit(solution)/shard_map/all_gather | solution.py:108
  289.6 6.6 %fusion.12 = bf16[1,1024,896]{2,1,0:T(8,128)(2,1)} fusion(bf16[1280,1024]{1,0:T(8,128)(2,1)} %all-gather.8.cloned.1.call-done, bf16[1280,896]{1,0:T(8,128)(2,1)} %bitcast.67), kind=kOutput, calls=%fused_computation.23 | convolution fusion | flops 2350645248 | bytes 6750208 | tf_op jit(solution)/shard_map/dot_general | solution.py:120
  296.2 2.9 all-to-all-done.5
  299.1 4.1 %fusion.19 = bf16[512,896]{1,0:T(8,128)(2,1)} fusion(bf16[1280,896]{1,0:T(8,128)(2,1)} %bitcast.23, s32[512]{0:T(512)S(1)} %get-tuple-element.33, s32[512]{0:T(512)S(1)} %get-tuple-element.32), kind=kOutput, calls=%fused_computation.27 | convolution fusion | flops 1176829952 | bytes 3215360 | tf_op jit(solution)/shard_map/dot_general | solution.py:123
  303.2 3.7 %all-to-all-start.6 = ((bf16[4,128,896]{2,1,0:T(8,128)(2,1)}), bf16[4,128,896]{2,1,0:T(8,128)(2,1)S(1)}, u32[]{:S(2)}, u32[]{:S(2)}) async-start(bf16[4,128,896]{2,1,0:T(8,128)(2,1)} %bitcast.72), calls=%async_computation.8 | async-start | bytes 1835008 | tf_op jit(solution)/shard_map/all_to_all | solution.py:34
  307.0 6.4 %fusion.6 = bf16[1,896,1024]{2,1,0:T(8,128)(2,1)} fusion(bf16[1280,896]{1,0:T(8,128)(2,1)} %bitcast.64, bf16[1280,2048]{1,0:T(8,128)(2,1)} %all-gather.6.cloned.1.call-done), kind=kOutput, calls=%fused_computation.19 | convolution fusion | flops 2350645248 | bytes 6750208 | tf_op jit(solution)/shard_map/dot_general | solution.py:117
  313.4 5.6 %fusion.5 = bf16[1,896,1024]{2,1,0:T(8,128)(2,1)} fusion(bf16[1280,896]{1,0:T(8,128)(2,1)S(1)} %bitcast.65, bf16[1280,2048]{1,0:T(8,128)(2,1)} %all-gather.6.cloned.1.call-done), kind=kOutput, calls=%fused_computation.18 | convolution fusion | flops 2350645248 | bytes 6750208 | tf_op jit(solution)/shard_map/dot_general | solution.py:117
  319.0 1.0 copy.53
  (43 shorter events, 0.6 us)
Async XLA Ops:
  7.2 148.5 %copy-start = (bf16[1,1024,896]{2,1,0:T(8,128)(2,1)S(1)}, bf16[1,1024,896]{2,1,0:T(8,128)(2,1)}, u32[]{:S(2)}) copy-start(bf16[1,1024,896]{2,1,0:T(8,128)(2,1)} %param.15) | copy-start | bytes 5505028
  7.2 8.2 %copy-start.5 = (s32[128,2]{0,1:T(2,128)S(1)}, s32[128,2]{0,1:T(2,128)}, u32[]{:S(2)}) copy-start(s32[128,2]{0,1:T(2,128)} %param.12) | copy-start | bytes 3076
  7.2 8.6 %copy-start.6 = (bf16[128,2]{0,1:T(2,128)(2,1)S(1)}, bf16[128,2]{0,1:T(2,128)(2,1)}, u32[]{:S(2)}) copy-start(bf16[128,2]{0,1:T(2,128)(2,1)} %param.11) | copy-start | bytes 1540
  9.5 22.0 %all-to-all-start.3 = ((bf16[4,128,896]{1,2,0:T(8,128)(2,1)}), bf16[4,128,896]{1,2,0:T(8,128)(2,1)S(1)}, u32[]{:S(2)}, u32[]{:S(2)}) async-start(bf16[4,128,896]{1,2,0:T(8,128)(2,1)} %bitcast.60), calls=%async_computation.4 | async-start | bytes 1835008 | tf_op jit(solution)/shard_map/all_to_all | solution.py:28
  15.4 158.6 %reduce-scatter.5.cloned.1.call-start = ((), (), s32[]{:S(2)}) async-start(), calls=%async_computation.11 | async-start | bytes 6553600 | tf_op jit(solution)/shard_map/reduce_scatter | solution.py:92
  35.5 42.9 %copy-start.7 = (bf16[1,896,1024]{2,1,0:T(8,128)(2,1)S(1)}, bf16[1,896,1024]{2,1,0:T(8,128)(2,1)}, u32[]{:S(2)}) copy-start(bf16[1,896,1024]{2,1,0:T(8,128)(2,1)} %param.14) | copy-start | bytes 5505028
  35.5 42.9 %copy-start.8 = (bf16[1,896,1024]{2,1,0:T(8,128)(2,1)S(1)}, bf16[1,896,1024]{2,1,0:T(8,128)(2,1)}, u32[]{:S(2)}) copy-start(bf16[1,896,1024]{2,1,0:T(8,128)(2,1)} %param.13) | copy-start | bytes 5505028
  77.0 1.4 copy-start.1
  86.0 1.2 copy-start.4
  86.0 104.0 %reduce-scatter.3.cloned.1.call-start = ((), (), s32[]{:S(2)}) async-start(), calls=%async_computation.10 | async-start | bytes 3276800 | tf_op jit(solution)/shard_map/reduce_scatter | solution.py:94
  154.3 1.4 copy-start.3
  160.0 0.7 copy-start.9
  160.0 0.7 copy-start.10
  163.0 10.8 %all-to-all-start = ((f32[32,1,41]{2,1,0:T(1,128)}), f32[32,1,41]{2,1,0:T(1,128)S(1)}, u32[]{:S(2)}, u32[]{:S(2)}) async-start(f32[32,1,41]{2,1,0:T(1,128)} %bitcast.7), calls=%async_computation | async-start | bytes 32768 | tf_op jit(solution)/shard_map/all_to_all | solution.py:39
  166.8 84.9 %all-gather.6.cloned.1.call-start = ((), (), s32[]{:S(2)}) async-start(), calls=%async_computation.12 | async-start | bytes 6553600 | tf_op jit(solution)/shard_map/all_gather | solution.py:107
  193.7 1.8 copy-start.11
  194.8 94.8 %all-gather.8.cloned.1.call-start = ((), (), s32[]{:S(2)}) async-start(), calls=%async_computation.13 | async-start | bytes 3276800 | tf_op jit(solution)/shard_map/all_gather | solution.py:108
  204.1 57.3 %all-to-all-start.7 = ((f32[32,1,40]{2,1,0:T(1,128)}), f32[32,1,40]{2,1,0:T(1,128)S(1)}, u32[]{:S(2)}, u32[]{:S(2)}) async-start(f32[32,1,40]{2,1,0:T(1,128)} %all_to_all.62), calls=%async_computation.9 | async-start | bytes 32768 | tf_op jit(solution)/shard_map/all_to_all | solution.py:39
  261.4 37.7 %all-to-all-start.5 = ((bf16[32,40,896]{2,1,0:T(8,128)(2,1)}), bf16[32,40,896]{2,1,0:T(8,128)(2,1)}, u32[]{:S(2)}, u32[]{:S(2)}) async-start(bf16[32,40,896]{2,1,0:T(8,128)(2,1)} %bitcast.68), calls=%async_computation.7 | async-start | bytes 4587520 | tf_op jit(solution)/shard_map/all_to_all | solution.py:39
  303.2 15.7 %all-to-all-start.6 = ((bf16[4,128,896]{2,1,0:T(8,128)(2,1)}), bf16[4,128,896]{2,1,0:T(8,128)(2,1)S(1)}, u32[]{:S(2)}, u32[]{:S(2)}) async-start(bf16[4,128,896]{2,1,0:T(8,128)(2,1)} %bitcast.72), calls=%async_computation.8 | async-start | bytes 1835008 | tf_op jit(solution)/shard_map/all_to_all | solution.py:34
  307.0 6.4 %copy-start.2 = (bf16[32,40,896]{2,1,0:T(8,128)(2,1)S(1)}, bf16[32,40,896]{2,1,0:T(8,128)(2,1)}, u32[]{:S(2)}) copy-start(bf16[32,40,896]{2,1,0:T(8,128)(2,1)} %copy-done.1) | copy-start | bytes 6881284
Sparse Core Ops, SparseCore 0:
  86.1 61.2 reduce-scatter.4
  160.1 29.7 reduce-scatter.2
  195.0 56.6 all-gather.5
  253.8 35.7 all-gather.7
